TPU v7x, 128 devices: a whole 4x4x4 slice. The times are simulated.
128 devices in a mesh: det: 4 (over y), tm: 32 (over x, z, core).
Axes of the slice: x: 4, y: 4, z: 4, core: 2. Of those that a mesh axis runs over, the one named last changes fastest.
Arguments:
- timestream: float32 [2048, 16384], P('det', 'tm'), may hold values from -18 to 18
- sample_flags: int32 [2048, 16384], P('det', 'tm'), may hold values 0 or 1
- pointing: bfloat16 [128, 4, 128, 128], P('tm'), may hold values from -0.5 to 0.5
- tile_ids: int32 [128, 4], P('tm'), may hold values from 0 to 127
- block_offsets: int32 [128, 4], P('tm'), may hold values from 0 to 127
- tile_owner: int32 [128], replicated, may hold values from 0 to 127, each once
- det_gains: float32 [2048], P('det'), may hold values from 0.5 to 2
- mode_vectors: float32 [2048, 32], P('det'), may hold values from -0.125 to 0.125
- filter_gain: float32 [257], replicated, may hold values from 0.05 to 1
Outputs:
- tile_snr: float32 [128, 128, 128], P(('det', 'tm'))
- cleaned: bfloat16 [2048, 16384], P('det', 'tm')
Inputs may be any that keep to these rules, and one draw needn't show every extreme that they name: Tile t is held in slot tile_owner[t]; slot q belongs to device q of det+tm in mesh order (one tile per device).
All inputs are finite; a program needn't handle non-finite values. No bound on the sum of `sample_flags` on one device may be relied on, other than what follows from the above.
Results may differ from a plain program's by a relative error of at most 0.0085.
Values may be sent and summed in bfloat16 or wider, within the bound.
A program may use at most 64 MiB of HBM per device.

v0:
```python
import math

import jax
import jax.numpy as jnp
from jax import lax
from jax.sharding import PartitionSpec as P

FLEN = 512
SEGLEN = 128
TILE = 128
BLOCKS_TILE = 128
TILES_DEV = 1


def spectral_tables():
    position = lax.iota(jnp.int32, FLEN)
    phase_index = position[:, None] * position[None, :] % FLEN
    angles = phase_index.astype(jnp.float32) * (2.0 * math.pi / FLEN)
    return (jnp.cos(angles).astype(jnp.bfloat16), jnp.sin(angles).astype(jnp.bfloat16))


def filter_rows(residual, response, forward, inverse):
    sample_rows = residual.astype(jnp.bfloat16)
    spectrum = jnp.dot(sample_rows, forward, preferred_element_type=jnp.float32)
    shaped = (spectrum * response[None, :]).astype(jnp.bfloat16)
    filtered = jnp.dot(shaped, inverse, preferred_element_type=jnp.float32) / FLEN
    return filtered


def shards(
    timestream,
    sample_flags,
    pointing,
    tile_ids,
    block_offsets,
    tile_owner,
    det_gains,
    mode_vectors,
    filter_gain,
):
    hi = lax.Precision.HIGHEST
    cosine, sine = spectral_tables()
    forward = jnp.concatenate([cosine, sine], axis=1)
    inverse = jnp.concatenate([cosine, sine], axis=0)
    full_gain = jnp.concatenate([filter_gain, filter_gain[1 : FLEN // 2][::-1]])
    response = jnp.concatenate([full_gain, full_gain])
    keep = (1 - sample_flags).astype(jnp.float32)
    seg_count, per_seg = tile_ids.shape
    listed = seg_count * per_seg
    tile_count = tile_owner.shape[0]
    tile_match = tile_ids[:, :, None] == lax.iota(jnp.int32, tile_count)[None, None, :]
    owner_slot = jnp.sum(jnp.where(tile_match, tile_owner[None, None, :], 0), axis=-1)
    target_rows = (owner_slot * BLOCKS_TILE + block_offsets).reshape(-1)
    squares = jnp.einsum("sktp,sktp->skp", pointing, pointing, preferred_element_type=jnp.float32)
    weights = (jnp.sum(det_gains * det_gains) * squares).reshape(listed, TILE)

    def clean_data(signal_rows):
        residual = (timestream - det_gains[:, None] * signal_rows[None, :]) * keep
        filtered = filter_rows(residual, response, forward, inverse)
        amplitudes = lax.psum(
            jnp.dot(mode_vectors.T, filtered, precision=hi).astype(jnp.bfloat16), "det"
        ).astype(jnp.float32)
        return filtered - jnp.dot(mode_vectors, amplitudes, precision=hi)

    def project(clean):
        summed = (
            jnp.dot(det_gains, clean, precision=hi).astype(jnp.bfloat16).reshape(seg_count, SEGLEN)
        )
        projected = jnp.einsum("sktp,st->skp", pointing, summed, preferred_element_type=jnp.float32)
        return projected.reshape(listed, TILE)

    def accumulate(values):
        onehot = (
            target_rows[:, None] == lax.iota(jnp.int32, tile_count * BLOCKS_TILE)[None, :]
        ).astype(jnp.float32)
        partial_value = jnp.einsum("lr,lc->rc", onehot, values, precision=hi)
        return lax.psum_scatter(partial_value, ("det", "tm"), scatter_dimension=0, tiled=True)

    first_clean = clean_data(jnp.zeros((timestream.shape[1],), jnp.float32))
    sums = accumulate(jnp.concatenate([project(first_clean), weights], axis=1))
    weight_sum = sums[:, TILE:] + 1.0
    map_rows = sums[:, :TILE] / weight_sum
    map_half = map_rows.astype(jnp.bfloat16)
    shard_part = lax.all_gather(map_half, ("det", "tm"), axis=0, tiled=True)
    onehot = (target_rows[:, None] == lax.iota(jnp.int32, shard_part.shape[0])[None, :]).astype(
        jnp.bfloat16
    )
    fetched = jnp.dot(onehot, shard_part, preferred_element_type=jnp.float32)
    fetched = fetched.astype(jnp.bfloat16).reshape(seg_count, per_seg, TILE)
    signal_rows = jnp.einsum(
        "sktp,skp->st", pointing, fetched, preferred_element_type=jnp.float32
    ).reshape(-1)
    second_clean = clean_data(signal_rows)
    second_sums = accumulate(project(second_clean))
    map_rows = map_rows + second_sums / weight_sum
    tile_snr = (map_rows * jnp.sqrt(weight_sum)).reshape(TILES_DEV, BLOCKS_TILE, TILE)
    return (tile_snr, second_clean.astype(jnp.bfloat16))


def solution(mesh):
    return jax.shard_map(
        shards,
        mesh=mesh,
        in_specs=(
            P("det", "tm"),
            P("det", "tm"),
            P("tm", None, None, None),
            P("tm", None),
            P("tm", None),
            P(),
            P("det"),
            P("det", None),
            P(),
        ),
        out_specs=(P(("det", "tm"), None, None), P("det", "tm")),
        check_vma=False,
    )
```

profile of v0, /device:TPU:1, one launch (start us, length us, event | category | flops | bytes accessed | tf_op | source)
XLA Modules:
  0.0 1469.4 jit_solution(17393306029124128783)
XLA Ops:
  7.2 0.0 copy-start
  7.2 0.0 reduce-scatter.3.cloned.1.call-start
  7.2 4.3 sine_convert_fusion
  11.5 0.8 slice.9
  12.3 0.1 reverse
  12.4 0.1 slice.28
  12.5 0.9 select_reduce_fusion
  13.4 0.7 multiply_add_fusion
  14.1 0.1 eq.19
  14.2 1.3 broadcast_multiply_fusion.1
  15.4 0.8 pad_maximum_fusion.8
  16.3 1.2 fusion.7
  17.4 2.9 convolution_multiply_fusion.1
  20.3 0.0 copy-done
  20.4 0.0 copy-start.3
  20.4 1.8 fusion.2
  22.2 0.0 copy-start.1
  22.2 15.8 %psum.14 = bf16[32,512]{0,1:T(8,128)(2,1)S(1)} all-reduce(bf16[32,512]{0,1:T(8,128)(2,1)S(1)} %fusion.2), channel_id=1, replica_groups=mesh['det'=4,'tm'=32] {'det'}, use_global_device_ids=true, to_apply=%region_1.2 | all-reduce | flops 16384 | bytes 65536 | tf_op jit(solution)/shard_map/psum | solution.py:60
  38.0 0.7 fusion.1
  38.7 0.0 copy-done.3
  38.7 0.6 fusion.48
  39.4 0.0 copy-done.1
  39.4 0.2 fusion.35
  39.6 0.7 broadcast_multiply_fusion
  40.2 9.8 fusion.13
  50.0 0.0 reduce-scatter.3.cloned.1.call-update
  50.0 0.0 all-gather.2.cloned.1.call-start
  50.1 662.7 %reduce-scatter.3.cloned.1.call-done = f32[128,256]{1,0:T(8,128)} async-done(((f32[16384,256]{1,0:T(8,128)}), f32[128,256]{1,0:T(8,128)}) %reduce-scatter.3.cloned.1.call-update) | async-done | bytes 131088 | tf_op jit(solution)/shard_map/reduce_scatter | solution.py:77
  712.8 1.5 fusion.46
  714.3 0.0 all-gather.2.cloned.1.call-update
  714.3 0.0 reduce-scatter.5.cloned.1.call-start
  714.4 70.1 %all-gather.2.cloned.1.call-done = bf16[16384,128]{1,0:T(8,128)(2,1)} async-done(((bf16[128,128]{1,0:T(8,128)(2,1)}), bf16[16384,128]{1,0:T(8,128)(2,1)}) %all-gather.2.cloned.1.call-update) | async-done | bytes 4194320 | tf_op jit(solution)/shard_map/all_gather | solution.py:84
  784.5 2.9 convolution_convert_fusion.2
  787.4 0.3 fusion.31
  787.7 2.9 convolution_multiply_fusion
  790.6 1.8 fusion.3
  792.4 13.0 psum.15
  805.4 1.5 fusion.47
  806.9 0.6 fusion.49
  807.5 0.2 fusion.33
  807.7 9.0 fusion.12
  816.7 0.0 copy-start.2
  816.7 0.0 reduce-scatter.5.cloned.1.call-update
  816.7 644.7 %reduce-scatter.5.cloned.1.call-done = f32[128,128]{1,0:T(8,128)} async-done(((f32[16384,128]{1,0:T(8,128)}), f32[128,128]{1,0:T(8,128)}) %reduce-scatter.5.cloned.1.call-update) | async-done | bytes 65552 | tf_op jit(solution)/shard_map/reduce_scatter | solution.py:77
  1461.4 0.0 copy-done.2
  1461.4 1.5 multiply_bitcast_fusion
  (2 shorter events, 0.0 us)
Async XLA Ops:
  7.2 13.2 copy-start
  7.2 705.6 %reduce-scatter.3.cloned.1.call-start = ((), (), s32[]{:S(2)}) async-start(), calls=%async_computation.2 | async-start | bytes 16908288 | tf_op jit(solution)/shard_map/reduce_scatter | solution.py:77
  20.4 18.4 %copy-start.3 = (f32[512]{0:T(512)S(1)}, f32[512]{0:T(512)}, u32[]{:S(2)}) copy-start(f32[512]{0:T(512)} %param.15) | copy-start | bytes 6148
  22.2 17.2 %copy-start.1 = (bf16[4,4,128,128]{3,2,1,0:T(8,128)(2,1)S(1)}, bf16[4,4,128,128]{3,2,1,0:T(8,128)(2,1)}, u32[]{:S(2)}) copy-start(bf16[4,4,128,128]{3,2,1,0:T(8,128)(2,1)} %param.11) | copy-start | bytes 1572868
  50.0 734.4 %all-gather.2.cloned.1.call-start = ((), (), s32[]{:S(2)}) async-start(), calls=%async_computation.3 | async-start | bytes 4227072 | tf_op jit(solution)/shard_map/all_gather | solution.py:84
  714.3 747.1 %reduce-scatter.5.cloned.1.call-start = ((), (), s32[]{:S(2)}) async-start(), calls=%async_computation.4 | async-start | bytes 8454144 | tf_op jit(solution)/shard_map/reduce_scatter | solution.py:77
  816.7 644.7 %copy-start.2 = (f32[128,256]{1,0:T(8,128)S(1)}, f32[128,256]{1,0:T(8,128)}, u32[]{:S(2)}) copy-start(f32[128,256]{1,0:T(8,128)} %reduce-scatter.3.cloned.1.call-done) | copy-start | bytes 393220
Sparse Core Ops, SparseCore 0:
  50.2 662.5 reduce-scatter.2
  716.5 67.9 all-gather.1
  816.8 644.5 reduce-scatter.4
where the time goes:
time: 1480 us; the launch traced here: 1470 us
  waiting for transfers between devices  1380 us (93%)
  matrix products  35.2 us (2%)
  blocking collectives  28.8 us (2%)
    reduce_scatter x2, waiting for transfers between devices, accumulate(): lax.psum_scatter(partial_value, ('det', 'tm'), scatter_dimension=0, tiled...  1310 us
    all_gather x1, waiting for transfers between devices, shards(): shard_part = lax.all_gather(map_half, ('det', 'tm'), axis=0, tiled=True)  70.1 us
  transfers between devices with their start and end apart: 3, of which 3 were waited for; matrix products, arithmetic and copies ran while one was open for 0% of the time, Pallas kernels for 0%

commit v1 on v0

v1 whole, which is shorter than its diff:
```python
import functools
import math

import jax
import jax.numpy as jnp
import ml_dtypes
import numpy as np
from jax import lax
from jax.experimental import pallas as pl
from jax.experimental.pallas import tpu as pltpu
from jax.sharding import PartitionSpec as P

FLEN = 512
HALF = FLEN // 2
TILE = 128
SEGLEN = 128
SEG_DEV = 4
KBLK = 4
LISTED = SEG_DEV * KBLK
MODES = 32
F32 = jnp.float32
BF16 = jnp.bfloat16
HI = lax.Precision.HIGHEST
MESH = pl.DeviceIdType.MESH
LAST = (((1,), (1,)), ((), ()))


def half_table():
    position = np.arange(FLEN)
    phase = position[:, None] * position[None, :] % FLEN
    angles = phase.astype(np.float32) * np.float32(2.0 * math.pi / FLEN)
    cosine, sine = np.cos(angles), np.sin(angles)
    table = np.concatenate([cosine[:, : HALF + 1], sine[:, 1:HALF]], axis=1)
    return table.astype(np.float32).astype(ml_dtypes.bfloat16)


def iota(shape, dim):
    return lax.broadcasted_iota(jnp.int32, shape, dim)


def halves(x):
    high = x.astype(BF16).astype(F32)
    return jnp.concatenate([high, x - high], axis=0).astype(BF16)


def folded(y):
    n = y.shape[0] // 2
    return y[:n] + y[n:]


def filter_rows(rows, table, response):
    spectrum = folded(jnp.dot(halves(rows), table, preferred_element_type=F32)) * response
    return folded(lax.dot_general(halves(spectrum), table, LAST, preferred_element_type=F32))


def kernel(
    n_det, n_tm,
    ts_hbm, fl_hbm, pt_hbm, table_hbm, tids, offs, owner, gains, modes, fgain,
    tile_out, clean_hbm,
    ts, fl, pt, table, clean, keepb, vpad, gcol, vcat,
    ubuf, rbuf, kbuf, bkbuf, wbuf, pbuf, qbuf,
    in_sem, out_sem, u_send, u_recv, r_send, r_recv, k_send, k_recv, bk_send, bk_recv,
    w_send, w_recv, p_send, p_recv, q_send, q_recv,
):
    det, tm = lax.axis_index("det"), lax.axis_index("tm")
    listed = n_tm * LISTED

    loads = []
    for n, (src, dst) in enumerate(((ts_hbm, ts), (fl_hbm, fl), (pt_hbm, pt), (table_hbm, table))):
        loads.append(pltpu.make_async_copy(src, dst, in_sem.at[n]))
        loads[-1].start()

    barrier = pltpu.get_barrier_semaphore()
    for d in range(1, n_det):
        pl.semaphore_signal(barrier, inc=1, device_id={"det": lax.rem(det + d, n_det)}, device_id_type=MESH)

    def greet(d, carry):
        pl.semaphore_signal(barrier, inc=1, device_id={"tm": lax.rem(tm + d, n_tm)}, device_id_type=MESH)
        return carry

    lax.fori_loop(1, n_tm, greet, 0)

    def det_copies(buf, send, recv):
        return [
            pltpu.make_async_remote_copy(
                src_ref=buf.at[0], dst_ref=buf.at[d], send_sem=send.at[d - 1], recv_sem=recv.at[d - 1],
                device_id={"det": lax.rem(det + d, n_det)}, device_id_type=MESH,
            )
            for d in range(1, n_det)
        ]

    def start(copies):
        for copy in copies:
            copy.start()

    def arrived(copies):
        for copy in copies:
            copy.wait_recv()

    def spread(buf, send, recv):
        def one(d, carry):
            pltpu.make_async_remote_copy(
                src_ref=buf.at[0], dst_ref=buf.at[d], send_sem=send, recv_sem=recv,
                device_id={"tm": lax.rem(tm + d, n_tm)}, device_id_type=MESH,
            ).start()
            return carry

        lax.fori_loop(1, n_tm, one, 0)

    def all_of(buf, sem):
        rest = buf.at[pl.ds(1, n_tm - 1)]
        pltpu.make_async_copy(rest, rest, sem).wait()

    g = gains[...]
    mode_rows = modes[...]
    vpad[...] = jnp.zeros_like(vpad)
    vpad[:, :MODES] = mode_rows
    vt = vpad[...].T[:MODES]
    ubuf[0] = jnp.zeros((8, 128), F32)
    ubuf[0, :, :MODES] = jnp.dot(
        jnp.broadcast_to(g, (8, g.shape[1])), mode_rows, precision=HI, preferred_element_type=F32
    )
    ubuf[0, :, MODES : 2 * MODES] = jnp.broadcast_to(jnp.sum(g * g, axis=1, keepdims=True), (8, MODES))

    pl.semaphore_wait(barrier, n_det - 1 + n_tm - 1)
    u_copies = det_copies(ubuf, u_send, u_recv)
    start(u_copies)

    first8 = iota((8, FLEN), 0) == 0
    weights = jnp.concatenate([vt, jnp.where(first8, g, 0.0)], axis=0)

    loads[0].wait()
    loads[1].wait()
    keep = (1 - fl[...]).astype(F32)
    keepb[...] = keep.astype(BF16)
    residual = (ts[...] * keep).astype(BF16)
    base = folded(jnp.dot(halves(weights), residual, preferred_element_type=F32))

    arrived(u_copies)
    usum = ubuf[0]
    for d in range(1, n_det):
        usum = usum + ubuf[d]
    u = usum[:, :MODES]
    squared_gain = usum[0:1, MODES : MODES + 1]

    def combine(rows):
        return rows[MODES : MODES + 1] - jnp.dot(u, rows[:MODES], precision=HI, preferred_element_type=F32)[0:1]

    rbuf[0] = combine(base)
    r_copies = det_copies(rbuf, r_send, r_recv)
    start(r_copies)

    loads[2].wait()
    pointing = pt[...].astype(F32)
    squares = jnp.sum((pointing * pointing).reshape(LISTED, SEGLEN, TILE), axis=1)
    lane16 = lax.rem(iota((1, 128), 1), LISTED)
    row16 = iota((LISTED, 128), 0)
    tile_row = jnp.zeros((1, 128), jnp.int32)
    off_row = jnp.zeros((1, 128), jnp.int32)
    own_key = jnp.zeros((LISTED, 128), jnp.int32)
    for n in range(LISTED):
        t, o = tids[n // KBLK, n % KBLK], offs[n // KBLK, n % KBLK]
        tile_row = jnp.where(lane16 == n, t, tile_row)
        off_row = jnp.where(lane16 == n, o, off_row)
        own_key = jnp.where(row16 == n, t * 128 + o, own_key)
    keys = jnp.where(row16 == 0, tile_row.astype(F32), jnp.where(row16 == 1, off_row.astype(F32), 0.0))
    wbuf[0] = jnp.concatenate([squares, keys], axis=0).astype(BF16)
    spread(wbuf, w_send, w_recv)

    kept = folded(jnp.dot(halves(weights * g), keepb[...], preferred_element_type=F32))
    kbuf[0] = combine(kept)
    k_copies = det_copies(kbuf, k_send, k_recv)
    start(k_copies)
    bkbuf[0] = jnp.concatenate([base[:MODES], kept[:MODES]], axis=0).astype(BF16)
    bk_copies = det_copies(bkbuf, bk_send, bk_recv)
    start(bk_copies)

    gain = fgain[...]
    low = gain[:, :HALF]
    lane_half = iota((1, HALF), 1)
    response = jnp.concatenate(
        [
            jnp.where(lane_half == 0, low * (1.0 / FLEN), low * (2.0 / FLEN)),
            jnp.where(lane_half == 0, gain[:, HALF : HALF + 1] * (1.0 / FLEN), low * (2.0 / FLEN)),
        ],
        axis=1,
    )

    def project(z):
        z_high = z.astype(BF16).astype(F32)
        rows = []
        for part in (z_high, z - z_high):
            blocks = []
            for n in range(LISTED):
                s = n // KBLK
                blocks.append(jnp.where(row16 == n, part[:, s * SEGLEN : (s + 1) * SEGLEN], 0.0))
            rows.append(jnp.concatenate(blocks, axis=1))
        lhs = jnp.concatenate(rows, axis=0).astype(BF16)
        return folded(jnp.dot(lhs, pt[...], preferred_element_type=F32))

    loads[3].wait()
    arrived(r_copies)
    r = rbuf[0]
    for d in range(1, n_det):
        r = r + rbuf[d]
    z = filter_rows(jnp.where(first8, r, 0.0), table[...], response)[0:1]
    pbuf[0] = project(z).astype(BF16)
    spread(pbuf, p_send, p_recv)

    gcol[...] = jnp.broadcast_to(g, (128, g.shape[1])).T
    vt_high = vt.astype(BF16).astype(F32)
    vt_low = vt - vt_high
    vcat[...] = jnp.concatenate([vt_high, vt_low, vt_high, jnp.zeros_like(vt)], axis=0).T.astype(BF16)
    all_of(wbuf, w_recv)
    info = wbuf[:, LISTED : 2 * LISTED, :].astype(F32)
    per = 128 // LISTED
    mine = iota((n_tm, LISTED, 128), 2) // LISTED == lax.rem(iota((n_tm, LISTED, 128), 0), per)
    info = jnp.sum(jnp.where(mine, info, 0.0).reshape(n_tm // per, per, LISTED, 128), axis=1)
    key = jnp.concatenate([info[c, 0:1] * 128.0 + info[c, 1:2] for c in range(n_tm // per)], axis=1)
    slot = det * n_tm + tm
    tile_mine = jnp.sum(
        jnp.where(owner[...] == slot, iota((1, 128), 1), 0).astype(F32), axis=1, keepdims=True
    )
    same = (own_key.astype(F32)[:, 0:1] == key).astype(F32).astype(BF16)
    into = (tile_mine * 128.0 + iota((128, listed), 0).astype(F32) == key).astype(F32).astype(BF16)
    all_squares = wbuf[:, :LISTED, :].reshape(listed, TILE)
    own_weight = 1.0 + squared_gain * jnp.dot(same, all_squares, preferred_element_type=F32)
    tile_weight = 1.0 + squared_gain * jnp.dot(into, all_squares, preferred_element_type=F32)
    arrived(k_copies)
    arrived(bk_copies)
    k = kbuf[0]
    bk = bkbuf[0].astype(F32)
    for d in range(1, n_det):
        k = k + kbuf[d]
        bk = bk + bkbuf[d].astype(F32)

    all_of(pbuf, p_recv)
    first = pbuf[...].reshape(listed, TILE)
    fetched = (jnp.dot(same, first, preferred_element_type=F32) / own_weight).astype(BF16)
    wide = lax.dot_general(fetched, pt[...], LAST, preferred_element_type=F32)
    diagonal = iota((LISTED, LISTED * SEGLEN), 0) == iota((LISTED, LISTED * SEGLEN), 1) // SEGLEN
    flat = jnp.sum(jnp.where(diagonal, wide, 0.0), axis=0, keepdims=True)
    parts = []
    for s in range(SEG_DEV):
        total = flat[:, s * KBLK * SEGLEN : (s * KBLK + 1) * SEGLEN]
        for n in range(s * KBLK + 1, (s + 1) * KBLK):
            total = total + flat[:, n * SEGLEN : (n + 1) * SEGLEN]
        parts.append(total)
    sig = jnp.concatenate(parts, axis=1)

    rows = jnp.concatenate([bk[:MODES] - sig * bk[MODES:], jnp.where(first8, r - sig * k, 0.0)], axis=0)
    rows = filter_rows(rows, table[...], response)
    qbuf[0] = project(rows[MODES : MODES + 1]).astype(BF16)
    spread(qbuf, q_send, q_recv)

    amp = rows[:MODES]
    amp_high = amp.astype(BF16).astype(F32)
    amp_cat = jnp.concatenate([amp_high, amp_high, amp - amp_high, jnp.zeros_like(amp)], axis=0).astype(BF16)
    chunk = 128

    def clean_rows(c, carry):
        at = pl.ds(pl.multiple_of(c * chunk, chunk), chunk)
        gains_here = jnp.concatenate([gcol[at, :]] * (FLEN // 128), axis=1)
        left = ((ts[at, :] - gains_here * sig) * keepb[at, :].astype(F32)).astype(BF16)
        shaped = (jnp.dot(left, table[...], preferred_element_type=F32) * response).astype(BF16)
        filtered = lax.dot_general(shaped, table[...], LAST, preferred_element_type=F32)
        filtered = filtered - jnp.dot(vcat[at, :], amp_cat, preferred_element_type=F32)
        clean[at, :] = filtered.astype(BF16)
        return carry

    lax.fori_loop(0, ts.shape[0] // chunk, clean_rows, 0)
    out = pltpu.make_async_copy(clean, clean_hbm, out_sem)
    out.start()
    sums = jnp.dot(into, first, preferred_element_type=F32) / tile_weight

    all_of(qbuf, q_recv)
    second = qbuf[...].reshape(listed, TILE)
    sums = sums + jnp.dot(into, second, preferred_element_type=F32) / tile_weight
    tile_out[...] = sums * jnp.sqrt(tile_weight)

    for copies in (u_copies, r_copies, k_copies, bk_copies):
        for copy in copies:
            copy.wait_send()
    all_of(wbuf, w_send)
    all_of(pbuf, p_send)
    all_of(qbuf, q_send)
    out.wait()


def solution(mesh):
    n_det, n_tm = mesh.shape["det"], mesh.shape["tm"]
    table_const = half_table()

    def shards(
        timestream, sample_flags, pointing, tile_ids, block_offsets, tile_owner, det_gains, mode_vectors, filter_gain
    ):
        dets, samples = timestream.shape
        anywhere = pl.BlockSpec(memory_space=pl.ANY)
        vmem = pl.BlockSpec(memory_space=pltpu.VMEM)
        smem = pl.BlockSpec(memory_space=pltpu.SMEM)
        dma = pltpu.SemaphoreType.DMA
        tile_snr, cleaned = pl.pallas_call(
            functools.partial(kernel, n_det, n_tm),
            out_shape=(
                jax.ShapeDtypeStruct((TILE, TILE), F32),
                jax.ShapeDtypeStruct((dets, samples), BF16),
            ),
            in_specs=[anywhere] * 4 + [smem] * 2 + [vmem] * 4,
            out_specs=(vmem, anywhere),
            scratch_shapes=[
                pltpu.VMEM((dets, samples), F32),
                pltpu.VMEM((dets, samples), jnp.int32),
                pltpu.VMEM((LISTED * SEGLEN, TILE), BF16),
                pltpu.VMEM((FLEN, FLEN), BF16),
                pltpu.VMEM((dets, samples), BF16),
                pltpu.VMEM((dets, samples), BF16),
                pltpu.VMEM((dets, 128), F32),
                pltpu.VMEM((dets, 128), F32),
                pltpu.VMEM((dets, 128), BF16),
                pltpu.VMEM((n_det, 8, 128), F32),
                pltpu.VMEM((n_det, 1, samples), F32),
                pltpu.VMEM((n_det, 1, samples), F32),
                pltpu.VMEM((n_det, 2 * MODES, samples), BF16),
                pltpu.VMEM((n_tm, 2 * LISTED, TILE), BF16),
                pltpu.VMEM((n_tm, LISTED, TILE), BF16),
                pltpu.VMEM((n_tm, LISTED, TILE), BF16),
                dma((4,)),
                dma,
            ]
            + [dma((n_det - 1,))] * 8
            + [dma] * 6,
            compiler_params=pltpu.CompilerParams(
                collective_id=0, has_side_effects=True, vmem_limit_bytes=40 * 1024 * 1024
            ),
        )(
            timestream,
            sample_flags,
            pointing.reshape(LISTED * SEGLEN, TILE),
            jnp.asarray(table_const),
            tile_ids,
            block_offsets,
            tile_owner.reshape(1, -1),
            det_gains.reshape(1, -1),
            mode_vectors,
            filter_gain.reshape(1, -1),
        )
        return tile_snr.reshape(1, TILE, TILE), cleaned

    return jax.shard_map(
        shards,
        mesh=mesh,
        in_specs=(
            P("det", "tm"), P("det", "tm"), P("tm", None, None, None), P("tm", None), P("tm", None),
            P(), P("det"), P("det", None), P(),
        ),
        out_specs=(P(("det", "tm"), None, None), P("det", "tm")),
        check_vma=False,
    )
```

time: 1480 us -> 37.5 us (0.03)
  waiting for transfers between devices: 1380 us -> 0 us
  matrix products: 35.2 us -> 0 us
  Pallas kernels: 0 us -> 28.8 us
  blocking collectives: 28.8 us -> 0 us
    reduce_scatter x2 -> x0, waiting for transfers between devices: 1310 us -> none  [accumulate(): lax.psum_scatter(partial_value, ('det', 'tm'), scatter_dimension=0, tiled...]
    all_gather x1 -> x0, waiting for transfers between devices: 70.1 us -> none  [shards(): shard_part = lax.all_gather(map_half, ('det', 'tm'), axis=0, tiled=True)]
    dot_general x14 -> x0, matrix products: 35.2 us -> none  [the longest x2 18.8 us: accumulate(): partial_value = jnp.einsum('lr,lc->rc', onehot, values, precision=hi)]
    psum x2 -> x0, blocking collectives: 28.8 us -> none  [clean_data(): lax.psum(jnp.dot(mode_vectors.T, filtered, precision=hi).astype(jnp.bfloa...]
    pallas_call x0 -> x1, Pallas kernels: none -> 28.8 us  [shards(): pl.pallas_call(functools.partial(kernel, n_det, n_tm), out_shape=(jax.Sha...]
  transfers between devices with their start and end apart: 3 -> 0, of which waited for: 3 -> 0; matrix products, arithmetic and copies ran while one was open for 0% -> 0% of each run, Pallas kernels for 0% -> 0%
where the time goes in v1:
time: 37.5 us; the launch traced here: 37.1 us
  Pallas kernels  28.8 us (77%)
  local copies, waits for them, and re-layouts  7.65 us (20%)
  between operations  0.71 us (2%)
    pallas_call x1, Pallas kernels, shards(): pl.pallas_call(functools.partial(kernel, n_det, n_tm), out_shape=(jax.Sha...  28.8 us
    unnamed x21, local copies, waits for them, and re-layouts  7.64 us

profile of v1, /device:TPU:1, one launch (start us, length us, event | category | flops | bytes accessed | tf_op | source)
XLA Modules:
  0.0 37.1 jit_solution(11705172351340330849)
XLA Ops:
  0.6 0.0 copy-start.8
  0.6 0.7 %copy-done.8 = f32[257]{0:T(512)S(1)} copy-done((f32[257]{0:T(512)S(1)}, f32[257]{0:T(512)}, u32[]{:S(2)}) %copy-start.8) | copy-done | bytes 1052
  1.3 0.0 copy-start.4
  1.3 0.0 copy-start.5
  1.3 0.0 copy-start.6
  1.3 0.0 copy-start.7
  1.3 1.0 %copy.12.modes = f32[512,32]{1,0:T(8,128)S(1)} copy(f32[512,32]{0,1:T(8,128)} %param.17) | data formatting | bytes 131072 | tf_op args[7]
  2.3 0.0 copy-done.4
  2.4 0.0 copy-done.5
  2.4 0.0 copy-done.6
  2.4 0.0 copy-done.7
  2.4 0.0 copy-start
  2.4 1.2 %copy-done = f32[512,512]{1,0:T(8,128)S(1)} copy-done((f32[512,512]{1,0:T(8,128)S(1)}, f32[512,512]{1,0:T(8,128)}, u32[]{:S(2)}) %copy-start) | copy-done | bytes 1048600
  3.6 0.0 copy-start.1
  3.6 1.2 %copy-done.1 = s32[512,512]{1,0:T(8,128)S(1)} copy-done((s32[512,512]{1,0:T(8,128)S(1)}, s32[512,512]{1,0:T(8,128)}, u32[]{:S(2)}) %copy-start.1) | copy-done | bytes 1048600
  4.8 0.0 copy-start.2
  4.8 1.0 %copy-done.2 = bf16[4,4,128,128]{3,2,1,0:T(8,128)(2,1)S(1)} copy-done((bf16[4,4,128,128]{3,2,1,0:T(8,128)(2,1)S(1)}, bf16[4,4,128,128]{3,2,1,0:T(8,128)(2,1)}, u32[]{:S(2)}) %copy-start.2) | copy-done | bytes 524312
  5.9 0.0 copy-start.3
  5.9 1.0 %copy-done.3 = bf16[512,512]{1,0:T(8,128)(2,1)S(1)} copy-done((bf16[512,512]{1,0:T(8,128)(2,1)S(1)}, bf16[512,512]{1,0:T(8,128)(2,1)}, u32[]{:S(2)}) %copy-start.3) | copy-done | bytes 524312
  6.9 28.8 %shard_map.113 = (f32[128,128]{1,0:T(8,128)S(1)}, bf16[512,512]{1,0:T(8,128)(2,1)S(1)}) custom-call(f32[512,512]{1,0:T(8,128)S(1)} %copy-done, s32[512,512]{1,0:T(8,128)S(1)} %copy-done.1, bf16[2048,128]{1,0:T(8,128)(2,1)S(1)} %bitcast.4, bf16[512,512]{1,0:T(8,128)(2,1)S(1)} %copy-done.3, s32[4,4]{1,0:T(4,128)S(1)} %copy-done.4, s32[4,4]{1,0:T(4,128)S(1)} %copy-done.5, ...), custom_call_target="tpu_custom_call" | custom-call | tf_op jit(solution)/shard_map/pallas_call | solution.py:302
  35.7 0.6 %copy.15 = f32[1,128,128]{2,1,0:T(8,128)} copy(f32[1,128,128]{2,1,0:T(8,128)S(1)} %bitcast.5) | data formatting | bytes 131072
  36.3 0.8 %copy.16 = bf16[512,512]{1,0:T(8,128)(2,1)} copy(bf16[512,512]{1,0:T(8,128)(2,1)S(1)} %get-tuple-element.9) | data formatting | bytes 1048576
  (1 shorter events, 0.0 us)
Async XLA Ops:
  0.6 0.7 %copy-start.8 = (f32[257]{0:T(512)S(1)}, f32[257]{0:T(512)}, u32[]{:S(2)}) copy-start(f32[257]{0:T(512)} %param.18) | copy-start | bytes 3088
  1.3 1.0 %copy-start.4 = (s32[4,4]{1,0:T(4,128)S(1)}, s32[4,4]{1,0:T(4,128)}, u32[]{:S(2)}) copy-start(s32[4,4]{1,0:T(4,128)} %tids.1) | copy-start | bytes 196
  1.3 1.0 %copy-start.5 = (s32[4,4]{1,0:T(4,128)S(1)}, s32[4,4]{1,0:T(4,128)}, u32[]{:S(2)}) copy-start(s32[4,4]{1,0:T(4,128)} %offs.1) | copy-start | bytes 196
  1.3 1.0 %copy-start.6 = (f32[512]{0:T(512)S(1)}, f32[512]{0:T(512)}, u32[]{:S(2)}) copy-start(f32[512]{0:T(512)} %param.16) | copy-start | bytes 6148
  1.3 1.1 %copy-start.7 = (s32[128]{0:T(128)S(1)}, s32[128]{0:T(128)}, u32[]{:S(2)}) copy-start(s32[128]{0:T(128)} %param.15) | copy-start | bytes 1540
  2.4 1.2 %copy-start = (f32[512,512]{1,0:T(8,128)S(1)}, f32[512,512]{1,0:T(8,128)}, u32[]{:S(2)}) copy-start(f32[512,512]{1,0:T(8,128)} %ts_hbm.1) | copy-start | bytes 3145732
  3.6 1.2 %copy-start.1 = (s32[512,512]{1,0:T(8,128)S(1)}, s32[512,512]{1,0:T(8,128)}, u32[]{:S(2)}) copy-start(s32[512,512]{1,0:T(8,128)} %fl_hbm.1) | copy-start | bytes 3145732
  4.8 1.0 %copy-start.2 = (bf16[4,4,128,128]{3,2,1,0:T(8,128)(2,1)S(1)}, bf16[4,4,128,128]{3,2,1,0:T(8,128)(2,1)}, u32[]{:S(2)}) copy-start(bf16[4,4,128,128]{3,2,1,0:T(8,128)(2,1)} %param.12) | copy-start | bytes 1572868
  5.9 1.0 %copy-start.3 = (bf16[512,512]{1,0:T(8,128)(2,1)S(1)}, bf16[512,512]{1,0:T(8,128)(2,1)}, u32[]{:S(2)}) copy-start(bf16[512,512]{1,0:T(8,128)(2,1)} %constant.2.clone.table_hbm) | copy-start | bytes 1572868

commit v2 on v1

v2 whole, which is shorter than its diff:
```python
import functools
import math

import jax
import jax.numpy as jnp
import ml_dtypes
import numpy as np
from jax import lax
from jax.experimental import pallas as pl
from jax.experimental.pallas import tpu as pltpu
from jax.sharding import PartitionSpec as P

FLEN = 512
HALF = FLEN // 2
TILE = 128
SEGLEN = 128
SEG_DEV = 4
KBLK = 4
LISTED = SEG_DEV * KBLK
MODES = 32
F32 = jnp.float32
BF16 = jnp.bfloat16
HI = lax.Precision.HIGHEST
MESH = pl.DeviceIdType.MESH
LAST = (((1,), (1,)), ((), ()))


def half_table():
    position = np.arange(FLEN)
    phase = position[:, None] * position[None, :] % FLEN
    angles = phase.astype(np.float32) * np.float32(2.0 * math.pi / FLEN)
    cosine, sine = np.cos(angles), np.sin(angles)
    table = np.concatenate([cosine[:, : HALF + 1], sine[:, 1:HALF]], axis=1)
    return table.astype(np.float32).astype(ml_dtypes.bfloat16)


def iota(shape, dim):
    return lax.broadcasted_iota(jnp.int32, shape, dim)


def halves(x):
    high = x.astype(BF16).astype(F32)
    return jnp.concatenate([high, x - high], axis=0).astype(BF16)


def folded(y):
    n = y.shape[0] // 2
    return y[:n] + y[n:]


def kernel(
    n_det, n_tm,
    gains_hbm, modes_hbm, fl_hbm, ts_hbm, pt_hbm, tids_hbm, offs_hbm, table_hbm, fgain_hbm, owner_hbm,
    tile_out, clean,
    gains, modes, fl, ts, pt, tids, offs, table, fgain, owner,
    keepb, gcol, vcat, table_t, pt_t, wide_filter,
    ybuf, xbuf, lbuf, kbuf, wbuf, pbuf, qbuf,
    in_sem, y_send, y_recv, x_send, x_recv, l_send, l_recv, k_send, k_recv,
    w_send, w_recv, p_send, p_recv, q_send, q_recv,
):
    det, tm = lax.axis_index("det"), lax.axis_index("tm")
    listed = n_tm * LISTED

    loads = []
    pairs = (
        (gains_hbm, gains), (modes_hbm, modes), (fl_hbm, fl), (ts_hbm, ts), (pt_hbm, pt),
        (tids_hbm, tids), (offs_hbm, offs), (table_hbm, table), (fgain_hbm, fgain), (owner_hbm, owner),
    )
    for n, (src, dst) in enumerate(pairs):
        loads.append(pltpu.make_async_copy(src, dst, in_sem.at[n]))
        loads[-1].start()

    n_z = 4
    n_x = n_tm // (2 * n_z)
    tm_x, tm_z, tm_core = tm // (2 * n_z), lax.rem(tm // 2, n_z), lax.rem(tm, 2)
    offsets = [(dx, dz, dc) for dx in range(n_x) for dz in range(n_z) for dc in range(2) if dx or dz or dc]
    offsets.sort(key=lambda o: -(min(o[0], n_x - o[0]) * 10 + min(o[1], n_z - o[1]) * 10 + o[2]))
    peers = []
    for dx, dz, dc in offsets:
        peer = (
            lax.rem(tm_x + dx, n_x) * (2 * n_z) + lax.rem(tm_z + dz, n_z) * 2 + lax.rem(tm_core + dc, 2)
        )
        peers.append((dx * 2 * n_z + dz * 2 + dc, {"tm": peer}))
    det_peers = [{"det": lax.rem(det + d, n_det)} for d in range(1, n_det)]

    barrier = pltpu.get_barrier_semaphore()
    for _, peer in peers:
        pl.semaphore_signal(barrier, inc=1, device_id=peer, device_id_type=MESH)
    for peer in det_peers:
        pl.semaphore_signal(barrier, inc=1, device_id=peer, device_id_type=MESH)

    def det_copies(buf, send, recv):
        return [
            pltpu.make_async_remote_copy(
                src_ref=buf.at[0], dst_ref=buf.at[d], send_sem=send.at[d - 1], recv_sem=recv.at[d - 1],
                device_id=det_peers[d - 1], device_id_type=MESH,
            )
            for d in range(1, n_det)
        ]

    def start(copies):
        for copy in copies:
            copy.start()

    def arrived(copies):
        for copy in copies:
            copy.wait_recv()

    def spread(buf, send, recv):
        for d, peer in peers:
            pltpu.make_async_remote_copy(
                src_ref=buf.at[0], dst_ref=buf.at[d], send_sem=send, recv_sem=recv,
                device_id=peer, device_id_type=MESH,
            ).start()

    def all_of(buf, sem):
        rest = buf.at[pl.ds(1, n_tm - 1)]
        pltpu.make_async_copy(rest, rest, sem).wait()

    loads[0].wait()
    loads[1].wait()
    g = gains[...]
    vt = modes[...]
    copies_u = jnp.concatenate(
        [lax.dot_general(jnp.broadcast_to(g, (8, g.shape[1])), vt, LAST, precision=HI, preferred_element_type=F32)]
        * n_det,
        axis=1,
    )[0:1]
    squared = jnp.broadcast_to(jnp.sum(g * g, axis=1, keepdims=True), (1, FLEN - n_det * MODES))
    first8 = iota((8, FLEN), 0) == 0
    weights = jnp.concatenate([vt, jnp.where(first8, g, 0.0)], axis=0)
    weight_halves = halves(weights)

    loads[2].wait()
    loads[3].wait()
    keep = (1 - fl[...]).astype(F32)
    keepb[...] = keep.astype(BF16)
    residual = (ts[...] * keep).astype(BF16)
    base = folded(jnp.dot(weight_halves, residual, preferred_element_type=F32))
    xbuf[0] = base[:MODES].astype(BF16)
    ybuf[0] = jnp.concatenate([base[MODES : MODES + 1], jnp.concatenate([copies_u, squared], axis=1)], axis=0)
    pl.semaphore_wait(barrier, n_det - 1 + n_tm - 1)
    x_copies = det_copies(xbuf, x_send, x_recv)
    y_copies = det_copies(ybuf, y_send, y_recv)
    start(x_copies)
    start(y_copies)

    for n in (4, 5, 6):
        loads[n].wait()
    pointing = pt[...].astype(F32)
    squares = jnp.sum((pointing * pointing).reshape(LISTED, SEGLEN, TILE), axis=1)
    lane16 = lax.rem(iota((1, 128), 1), LISTED)
    row16 = iota((LISTED, 128), 0)
    tile_row = jnp.zeros((1, 128), jnp.int32)
    off_row = jnp.zeros((1, 128), jnp.int32)
    own_key = jnp.zeros((LISTED, 128), jnp.int32)
    for n in range(LISTED):
        t, o = tids[n // KBLK, n % KBLK], offs[n // KBLK, n % KBLK]
        tile_row = jnp.where(lane16 == n, t, tile_row)
        off_row = jnp.where(lane16 == n, o, off_row)
        own_key = jnp.where(row16 == n, t * 128 + o, own_key)
    keys = jnp.where(row16 == 0, tile_row.astype(F32), jnp.where(row16 == 1, off_row.astype(F32), 0.0))
    wbuf[0] = jnp.concatenate([squares, keys], axis=0).astype(BF16)
    spread(wbuf, w_send, w_recv)

    kept = folded(jnp.dot(halves(weights * g), keepb[...], preferred_element_type=F32))
    lbuf[0] = kept[:MODES].astype(BF16)
    kbuf[0] = kept[MODES : MODES + 1]
    l_copies = det_copies(lbuf, l_send, l_recv)
    k_copies = det_copies(kbuf, k_send, k_recv)
    start(l_copies)
    start(k_copies)

    loads[8].wait()
    gain = fgain[...].reshape(1, HALF + 1)
    low = gain[:, :HALF]
    lane_half = iota((1, HALF), 1)
    response = jnp.concatenate(
        [
            jnp.where(lane_half == 0, low * (1.0 / FLEN), low * (2.0 / FLEN)),
            jnp.where(lane_half == 0, gain[:, HALF : HALF + 1] * (1.0 / FLEN), low * (2.0 / FLEN)),
        ],
        axis=1,
    )
    loads[7].wait()
    table_t[...] = table[...].T
    scaled = table[...].astype(F32) * response
    scaled_high = scaled.astype(BF16)
    scaled_low = (scaled - scaled_high.astype(F32)).astype(BF16)
    whole = jnp.dot(scaled_high, table_t[...], preferred_element_type=F32)
    whole = whole + jnp.dot(scaled_low, table_t[...], preferred_element_type=F32)
    whole_high = whole.astype(BF16)
    wide_filter[:, :FLEN] = whole_high
    wide_filter[:, FLEN:] = (whole - whole_high.astype(F32)).astype(BF16)

    def filter_rows(rows):
        both = jnp.dot(halves(rows), wide_filter[...], preferred_element_type=F32)
        n = rows.shape[0]
        return both[:n, :FLEN] + both[n:, :FLEN] + both[:n, FLEN:]

    def project(z):
        z_high = z.astype(BF16).astype(F32)
        rows = []
        for part in (z_high, z - z_high):
            blocks = []
            for n in range(LISTED):
                s = n // KBLK
                blocks.append(jnp.where(row16 == n, part[:, s * SEGLEN : (s + 1) * SEGLEN], 0.0))
            rows.append(jnp.concatenate(blocks, axis=1))
        lhs = jnp.concatenate(rows, axis=0).astype(BF16)
        return folded(jnp.dot(lhs, pt[...], preferred_element_type=F32))

    arrived(x_copies)
    arrived(y_copies)
    y = ybuf[0]
    for d in range(1, n_det):
        y = y + ybuf[d]
    u = halves(jnp.broadcast_to(y[1:2, : n_det * MODES], (8, n_det * MODES)))
    squared_gain = y[1:2, FLEN - 1 : FLEN]

    def combine(total, group_rows):
        return total - folded(
            jnp.dot(u, group_rows[...].reshape(n_det * MODES, FLEN), preferred_element_type=F32)
        )

    r = combine(y[0:1], xbuf)
    pbuf[0] = project(filter_rows(r)[0:1]).astype(BF16)
    spread(pbuf, p_send, p_recv)

    for n in range(LISTED):
        pt_t[:, n * SEGLEN : (n + 1) * SEGLEN] = pt[n * SEGLEN : (n + 1) * SEGLEN, :].T
    gcol[...] = jnp.broadcast_to(g, (128, g.shape[1])).T
    vt_high = vt.astype(BF16).astype(F32)
    vt_low = vt - vt_high
    vcat[...] = jnp.concatenate([vt_high, vt_low, vt_high, jnp.zeros_like(vt)], axis=0).T.astype(BF16)
    arrived(l_copies)
    arrived(k_copies)
    k = kbuf[0]
    base_sum = xbuf[0].astype(F32)
    kept_sum = lbuf[0].astype(F32)
    for d in range(1, n_det):
        k = k + kbuf[d]
        base_sum = base_sum + xbuf[d].astype(F32)
        kept_sum = kept_sum + lbuf[d].astype(F32)
    k = combine(k, lbuf)
    all_of(wbuf, w_recv)
    info = wbuf[:, LISTED : 2 * LISTED, :].astype(F32)
    per = 128 // LISTED
    mine = iota((n_tm, LISTED, 128), 2) // LISTED == lax.rem(iota((n_tm, LISTED, 128), 0), per)
    info = jnp.sum(jnp.where(mine, info, 0.0).reshape(n_tm // per, per, LISTED, 128), axis=1)
    key = jnp.concatenate([info[c, 0:1] * 128.0 + info[c, 1:2] for c in range(n_tm // per)], axis=1)
    slot = det * n_tm + tm
    loads[9].wait()
    tile_mine = jnp.sum(
        jnp.where(owner[...] == slot, iota((1, 128), 1), 0).astype(F32), axis=1, keepdims=True
    )
    same = (own_key.astype(F32)[:, 0:1] == key).astype(F32).astype(BF16)
    into = (tile_mine * 128.0 + iota((128, listed), 0).astype(F32) == key).astype(F32).astype(BF16)
    all_squares = wbuf[:, :LISTED, :].reshape(listed, TILE)
    own_scale = 1.0 / (1.0 + squared_gain * jnp.dot(same, all_squares, preferred_element_type=F32))
    tile_weight = 1.0 + squared_gain * jnp.dot(into, all_squares, preferred_element_type=F32)
    tile_scale = jnp.sqrt(tile_weight) / tile_weight

    all_of(pbuf, p_recv)
    first = pbuf[...].reshape(listed, TILE)
    fetched = (jnp.dot(same, first, preferred_element_type=F32) * own_scale).astype(BF16)
    wide = jnp.dot(fetched, pt_t[...], preferred_element_type=F32)
    diagonal = iota((LISTED, LISTED * SEGLEN), 0) == iota((LISTED, LISTED * SEGLEN), 1) // SEGLEN
    flat = jnp.sum(jnp.where(diagonal, wide, 0.0), axis=0, keepdims=True)
    parts = []
    for s in range(SEG_DEV):
        total = flat[:, s * KBLK * SEGLEN : (s * KBLK + 1) * SEGLEN]
        for n in range(s * KBLK + 1, (s + 1) * KBLK):
            total = total + flat[:, n * SEGLEN : (n + 1) * SEGLEN]
        parts.append(total)
    sig = jnp.concatenate(parts, axis=1)
    qbuf[0] = project(filter_rows(r - sig * k)[0:1]).astype(BF16)
    spread(qbuf, q_send, q_recv)

    amp = filter_rows(base_sum - sig * kept_sum)
    amp_high = amp.astype(BF16).astype(F32)
    amp_cat = jnp.concatenate([amp_high, amp_high, amp - amp_high, jnp.zeros_like(amp)], axis=0).astype(BF16)
    chunk = 128

    def clean_rows(c, carry):
        at = pl.ds(pl.multiple_of(c * chunk, chunk), chunk)
        gains_here = jnp.concatenate([gcol[at, :]] * (FLEN // 128), axis=1)
        left = ((ts[at, :] - gains_here * sig) * keepb[at, :].astype(F32)).astype(BF16)
        shaped = (jnp.dot(left, table[...], preferred_element_type=F32) * response).astype(BF16)
        filtered = jnp.dot(shaped, table_t[...], preferred_element_type=F32)
        filtered = filtered - jnp.dot(vcat[at, :], amp_cat, preferred_element_type=F32)
        clean[at, :] = filtered.astype(BF16)
        return carry

    lax.fori_loop(0, ts.shape[0] // chunk, clean_rows, 0)
    sums = jnp.dot(into, first, preferred_element_type=F32)

    all_of(qbuf, q_recv)
    second = qbuf[...].reshape(listed, TILE)
    sums = sums + jnp.dot(into, second, preferred_element_type=F32)
    tile_out[...] = sums * tile_scale

    for copies in (x_copies, y_copies, l_copies, k_copies):
        for copy in copies:
            copy.wait_send()
    all_of(wbuf, w_send)
    all_of(pbuf, p_send)
    all_of(qbuf, q_send)


def solution(mesh):
    n_det, n_tm = mesh.shape["det"], mesh.shape["tm"]
    table_const = half_table()

    def shards(
        timestream, sample_flags, pointing, tile_ids, block_offsets, tile_owner, det_gains, mode_vectors, filter_gain
    ):
        dets, samples = timestream.shape
        hbm = pl.BlockSpec(memory_space=pltpu.HBM)
        vmem = pl.BlockSpec(memory_space=pltpu.VMEM)
        dma = pltpu.SemaphoreType.DMA
        tile_snr, cleaned = pl.pallas_call(
            functools.partial(kernel, n_det, n_tm),
            out_shape=(
                jax.ShapeDtypeStruct((TILE, TILE), F32),
                jax.ShapeDtypeStruct((dets, samples), BF16),
            ),
            in_specs=[hbm] * 10,
            out_specs=(vmem, vmem),
            scratch_shapes=[
                pltpu.VMEM((1, dets), F32),
                pltpu.VMEM((MODES, dets), F32),
                pltpu.VMEM((dets, samples), jnp.int32),
                pltpu.VMEM((dets, samples), F32),
                pltpu.VMEM((LISTED * SEGLEN, TILE), BF16),
                pltpu.SMEM((SEG_DEV, KBLK), jnp.int32),
                pltpu.SMEM((SEG_DEV, KBLK), jnp.int32),
                pltpu.VMEM((FLEN, FLEN), BF16),
                pltpu.VMEM((HALF + 1,), F32),
                pltpu.VMEM((1, tile_owner.shape[0]), jnp.int32),
                pltpu.VMEM((dets, samples), BF16),
                pltpu.VMEM((dets, 128), F32),
                pltpu.VMEM((dets, 128), BF16),
                pltpu.VMEM((FLEN, FLEN), BF16),
                pltpu.VMEM((TILE, LISTED * SEGLEN), BF16),
                pltpu.VMEM((FLEN, 2 * FLEN), BF16),
                pltpu.VMEM((n_det, 2, samples), F32),
                pltpu.VMEM((n_det, MODES, samples), BF16),
                pltpu.VMEM((n_det, MODES, samples), BF16),
                pltpu.VMEM((n_det, 1, samples), F32),
                pltpu.VMEM((n_tm, 2 * LISTED, TILE), BF16),
                pltpu.VMEM((n_tm, LISTED, TILE), BF16),
                pltpu.VMEM((n_tm, LISTED, TILE), BF16),
                dma((10,)),
            ]
            + [dma((n_det - 1,))] * 8
            + [dma] * 6,
            compiler_params=pltpu.CompilerParams(
                collective_id=0, has_side_effects=True, vmem_limit_bytes=40 * 1024 * 1024
            ),
        )(
            *(
                pltpu.with_memory_space_constraint(operand, pltpu.HBM)
                for operand in (
                    det_gains.reshape(1, -1),
                    mode_vectors.T,
                    sample_flags,
                    timestream,
                    pointing.reshape(LISTED * SEGLEN, TILE),
                    tile_ids,
                    block_offsets,
                    jnp.asarray(table_const),
                    filter_gain,
                    tile_owner.reshape(1, -1),
                )
            )
        )
        return tile_snr.reshape(1, TILE, TILE), cleaned

    return jax.shard_map(
        shards,
        mesh=mesh,
        in_specs=(
            P("det", "tm"), P("det", "tm"), P("tm", None, None, None), P("tm", None), P("tm", None),
            P(), P("det"), P("det", None), P(),
        ),
        out_specs=(P(("det", "tm"), None, None), P("det", "tm")),
        check_vma=False,
    )
```

time: 37.5 us -> 27.5 us (0.73)
  local copies, waits for them, and re-layouts: 7.65 us -> 1.42 us
  Pallas kernels: 28.8 us -> 25.3 us
    unnamed x21 -> x2, local copies, waits for them, and re-layouts: 7.64 us -> 1.42 us
    pallas_call x1, Pallas kernels: 28.8 us -> 25.3 us  [shards(): pl.pallas_call(functools.partial(kernel, n_det, n_tm), out_shape=(jax.Sha...]
where the time goes in v2:
time: 27.5 us; the launch traced here: 27.4 us
  Pallas kernels  25.3 us (92%)
  local copies, waits for them, and re-layouts  1.42 us (5%)
  between operations  0.64 us (2%)
    pallas_call x1, Pallas kernels, shards(): pl.pallas_call(functools.partial(kernel, n_det, n_tm), out_shape=(jax.Sha...  25.3 us
    unnamed x2, local copies, waits for them, and re-layouts  1.42 us

profile of v2, /device:TPU:1, one launch (start us, length us, event | category | flops | bytes accessed | tf_op | source)
XLA Modules:
  0.0 27.4 jit_solution(147795631495141452)
XLA Ops:
  0.6 25.3 %shard_map.113 = (f32[128,128]{1,0:T(8,128)S(1)}, bf16[512,512]{1,0:T(8,128)(2,1)S(1)}) custom-call(f32[1,512]{1,0:T(1,128)} %bitcast.8, f32[32,512]{1,0:T(8,128)} %bitcast.7, s32[512,512]{1,0:T(8,128)} %fl_hbm.1, f32[512,512]{1,0:T(8,128)} %ts_hbm.1, bf16[2048,128]{1,0:T(8,128)(2,1)} %bitcast.6, s32[4,4]{1,0:T(4,128)} %tids_hbm.1, s32[4,4]{1,0:T(4,128)} %offs_hbm.1, ...), custom_call_target="tpu_custom_call" | custom-call | tf_op jit(solution)/shard_map/pallas_call | solution.py:322
  25.9 0.6 %copy.14 = f32[1,128,128]{2,1,0:T(8,128)} copy(f32[1,128,128]{2,1,0:T(8,128)S(1)} %bitcast.5) | data formatting | bytes 131072
  26.6 0.8 %copy.15 = bf16[512,512]{1,0:T(8,128)(2,1)} copy(bf16[512,512]{1,0:T(8,128)(2,1)S(1)} %get-tuple-element.9) | data formatting | bytes 1048576

commit v3 on v2

--- a/solution.py
+++ b/solution.py
@@ -55,7 +55,7 @@
     gains, modes, fl, ts, pt, tids, offs, table, fgain, owner,
     keepb, gcol, vcat, table_t, pt_t, wide_filter,
     ybuf, xbuf, lbuf, kbuf, wbuf, pbuf, qbuf,
-    in_sem, y_send, y_recv, x_send, x_recv, l_send, l_recv, k_send, k_recv,
+    column_sem, in_sem, y_send, y_recv, x_send, x_recv, l_send, l_recv, k_send, k_recv,
     w_send, w_recv, p_send, p_recv, q_send, q_recv,
 ):
     det, tm = lax.axis_index("det"), lax.axis_index("tm")
@@ -84,9 +84,10 @@
     det_peers = [{"det": lax.rem(det + d, n_det)} for d in range(1, n_det)]
 
     barrier = pltpu.get_barrier_semaphore()
-    for _, peer in peers:
-        pl.semaphore_signal(barrier, inc=1, device_id=peer, device_id_type=MESH)
-    for peer in det_peers:
+    row_peers = [peer for (dx, dz, dc), (_, peer) in zip(offsets, peers) if dz == 0 and dc == 0]
+    column_peers = [peer for (dx, dz, dc), (_, peer) in zip(offsets, peers) if dx == 0]
+    near = det_peers + row_peers + column_peers
+    for peer in near:
         pl.semaphore_signal(barrier, inc=1, device_id=peer, device_id_type=MESH)
 
     def det_copies(buf, send, recv):
@@ -139,7 +140,9 @@
     base = folded(jnp.dot(weight_halves, residual, preferred_element_type=F32))
     xbuf[0] = base[:MODES].astype(BF16)
     ybuf[0] = jnp.concatenate([base[MODES : MODES + 1], jnp.concatenate([copies_u, squared], axis=1)], axis=0)
-    pl.semaphore_wait(barrier, n_det - 1 + n_tm - 1)
+    pl.semaphore_wait(barrier, len(near))
+    for peer in row_peers:
+        pl.semaphore_signal(column_sem, inc=1, device_id=peer, device_id_type=MESH)
     x_copies = det_copies(xbuf, x_send, x_recv)
     y_copies = det_copies(ybuf, y_send, y_recv)
     start(x_copies)
@@ -161,6 +164,7 @@
         own_key = jnp.where(row16 == n, t * 128 + o, own_key)
     keys = jnp.where(row16 == 0, tile_row.astype(F32), jnp.where(row16 == 1, off_row.astype(F32), 0.0))
     wbuf[0] = jnp.concatenate([squares, keys], axis=0).astype(BF16)
+    pl.semaphore_wait(column_sem, len(row_peers))
     spread(wbuf, w_send, w_recv)
 
     kept = folded(jnp.dot(halves(weights * g), keepb[...], preferred_element_type=F32))
@@ -351,6 +355,7 @@
                 pltpu.VMEM((n_tm, 2 * LISTED, TILE), BF16),
                 pltpu.VMEM((n_tm, LISTED, TILE), BF16),
                 pltpu.VMEM((n_tm, LISTED, TILE), BF16),
+                pltpu.SemaphoreType.REGULAR,
                 dma((10,)),
             ]
             + [dma((n_det - 1,))] * 8

time: 27.5 us -> 25.4 us (0.924)
  Pallas kernels: 25.3 us -> 23.2 us
    pallas_call x1, Pallas kernels: 25.3 us -> 23.2 us  [shards(): pl.pallas_call(functools.partial(kernel, n_det, n_tm), out_shape=(jax.Sha...]
where the time goes in v3:
time: 25.4 us; the launch traced here: 25.3 us
  Pallas kernels  23.2 us (91%)
  local copies, waits for them, and re-layouts  1.42 us (6%)
  between operations  0.64 us (3%)
    pallas_call x1, Pallas kernels, shards(): pl.pallas_call(functools.partial(kernel, n_det, n_tm), out_shape=(jax.Sha...  23.2 us
    unnamed x2, local copies, waits for them, and re-layouts  1.42 us

profile of v3, /device:TPU:1, one launch (start us, length us, event | category | flops | bytes accessed | tf_op | source)
XLA Modules:
  0.0 25.3 jit_solution(13728431193986581980)
XLA Ops:
  0.6 23.2 %shard_map.113 = (f32[128,128]{1,0:T(8,128)S(1)}, bf16[512,512]{1,0:T(8,128)(2,1)S(1)}) custom-call(f32[1,512]{1,0:T(1,128)} %bitcast.8, f32[32,512]{1,0:T(8,128)} %bitcast.7, s32[512,512]{1,0:T(8,128)} %fl_hbm.1, f32[512,512]{1,0:T(8,128)} %ts_hbm.1, bf16[2048,128]{1,0:T(8,128)(2,1)} %bitcast.6, s32[4,4]{1,0:T(4,128)} %tids_hbm.1, s32[4,4]{1,0:T(4,128)} %offs_hbm.1, ...), custom_call_target="tpu_custom_call" | custom-call | tf_op jit(solution)/shard_map/pallas_call | solution.py:326
  23.9 0.6 %copy.14 = f32[1,128,128]{2,1,0:T(8,128)} copy(f32[1,128,128]{2,1,0:T(8,128)S(1)} %bitcast.5) | data formatting | bytes 131072
  24.5 0.8 %copy.15 = bf16[512,512]{1,0:T(8,128)(2,1)} copy(bf16[512,512]{1,0:T(8,128)(2,1)S(1)} %get-tuple-element.9) | data formatting | bytes 1048576

commit v4 on v3

--- a/solution.py
+++ b/solution.py
@@ -54,9 +54,9 @@
     tile_out, clean,
     gains, modes, fl, ts, pt, tids, offs, table, fgain, owner,
     keepb, gcol, vcat, table_t, pt_t, wide_filter,
-    ybuf, xbuf, lbuf, kbuf, wbuf, pbuf, qbuf,
-    column_sem, in_sem, y_send, y_recv, x_send, x_recv, l_send, l_recv, k_send, k_recv,
-    w_send, w_recv, p_send, p_recv, q_send, q_recv,
+    ybuf, xbuf, lbuf, kbuf, wbuf, idbuf, pbuf, qbuf,
+    column_sem, core_sem, share_send, share_recv, in_sem, y_send, y_recv, x_send, x_recv, l_send, l_recv, k_send, k_recv,
+    w_send, w_recv, id_send, id_recv, p_send, p_recv, q_send, q_recv,
 ):
     det, tm = lax.axis_index("det"), lax.axis_index("tm")
     listed = n_tm * LISTED
@@ -72,6 +72,7 @@
 
     n_z = 4
     n_x = n_tm // (2 * n_z)
+    half = n_tm // 2
     tm_x, tm_z, tm_core = tm // (2 * n_z), lax.rem(tm // 2, n_z), lax.rem(tm, 2)
     offsets = [(dx, dz, dc) for dx in range(n_x) for dz in range(n_z) for dc in range(2) if dx or dz or dc]
     offsets.sort(key=lambda o: -(min(o[0], n_x - o[0]) * 10 + min(o[1], n_z - o[1]) * 10 + o[2]))
@@ -80,13 +81,15 @@
         peer = (
             lax.rem(tm_x + dx, n_x) * (2 * n_z) + lax.rem(tm_z + dz, n_z) * 2 + lax.rem(tm_core + dc, 2)
         )
-        peers.append((dx * 2 * n_z + dz * 2 + dc, {"tm": peer}))
+        peers.append((dc * half + dx * n_z + dz, {"tm": peer}))
     det_peers = [{"det": lax.rem(det + d, n_det)} for d in range(1, n_det)]
 
     barrier = pltpu.get_barrier_semaphore()
-    row_peers = [peer for (dx, dz, dc), (_, peer) in zip(offsets, peers) if dz == 0 and dc == 0]
-    column_peers = [peer for (dx, dz, dc), (_, peer) in zip(offsets, peers) if dx == 0]
-    near = det_peers + row_peers + column_peers
+    row_peers = [peer for (_, dz, dc), (_, peer) in zip(offsets, peers) if dz == 0 and dc == 0]
+    column_peers = [peer for (dx, _, dc), (_, peer) in zip(offsets, peers) if dx == 0 and dc == 0]
+    plane_peers = [pair for (_, _, dc), pair in zip(offsets, peers) if dc == 0]
+    sibling = {"tm": tm + 1 - 2 * tm_core}
+    near = column_peers + det_peers + row_peers + [sibling]
     for peer in near:
         pl.semaphore_signal(barrier, inc=1, device_id=peer, device_id_type=MESH)
 
@@ -107,15 +110,15 @@
         for copy in copies:
             copy.wait_recv()
 
-    def spread(buf, send, recv):
-        for d, peer in peers:
+    def spread(buf, send, recv, to):
+        for d, peer in to:
             pltpu.make_async_remote_copy(
                 src_ref=buf.at[0], dst_ref=buf.at[d], send_sem=send, recv_sem=recv,
                 device_id=peer, device_id_type=MESH,
             ).start()
 
-    def all_of(buf, sem):
-        rest = buf.at[pl.ds(1, n_tm - 1)]
+    def all_of(buf, sem, count=n_tm - 1):
+        rest = buf.at[pl.ds(1, count)]
         pltpu.make_async_copy(rest, rest, sem).wait()
 
     loads[0].wait()
@@ -154,18 +157,18 @@
     squares = jnp.sum((pointing * pointing).reshape(LISTED, SEGLEN, TILE), axis=1)
     lane16 = lax.rem(iota((1, 128), 1), LISTED)
     row16 = iota((LISTED, 128), 0)
-    tile_row = jnp.zeros((1, 128), jnp.int32)
-    off_row = jnp.zeros((1, 128), jnp.int32)
+    key_row = jnp.zeros((1, 128), jnp.int32)
     own_key = jnp.zeros((LISTED, 128), jnp.int32)
     for n in range(LISTED):
-        t, o = tids[n // KBLK, n % KBLK], offs[n // KBLK, n % KBLK]
-        tile_row = jnp.where(lane16 == n, t, tile_row)
-        off_row = jnp.where(lane16 == n, o, off_row)
-        own_key = jnp.where(row16 == n, t * 128 + o, own_key)
-    keys = jnp.where(row16 == 0, tile_row.astype(F32), jnp.where(row16 == 1, off_row.astype(F32), 0.0))
-    wbuf[0] = jnp.concatenate([squares, keys], axis=0).astype(BF16)
+        own = tids[n // KBLK, n % KBLK] * 128 + offs[n // KBLK, n % KBLK]
+        key_row = jnp.where(lane16 == n, own, key_row)
+        own_key = jnp.where(row16 == n, own, own_key)
+    wbuf[0] = squares.astype(BF16)
+    idbuf[0] = key_row.astype(F32)
     pl.semaphore_wait(column_sem, len(row_peers))
-    spread(wbuf, w_send, w_recv)
+    pl.semaphore_signal(core_sem, inc=1, device_id=sibling, device_id_type=MESH)
+    spread(wbuf, w_send, w_recv, plane_peers)
+    spread(idbuf, id_send, id_recv, plane_peers)
 
     kept = folded(jnp.dot(halves(weights * g), keepb[...], preferred_element_type=F32))
     lbuf[0] = kept[:MODES].astype(BF16)
@@ -229,8 +232,19 @@
 
     r = combine(y[0:1], xbuf)
     pbuf[0] = project(filter_rows(r)[0:1]).astype(BF16)
-    spread(pbuf, p_send, p_recv)
-
+    pl.semaphore_wait(core_sem, 1)
+    spread(pbuf, p_send, p_recv, peers)
+
+    all_of(wbuf, w_recv, half - 1)
+    all_of(idbuf, id_recv, half - 1)
+    shares = [
+        pltpu.make_async_remote_copy(
+            src_ref=buf.at[pl.ds(0, half)], dst_ref=buf.at[pl.ds(half, half)],
+            send_sem=share_send.at[n], recv_sem=share_recv.at[n], device_id=sibling, device_id_type=MESH,
+        )
+        for n, buf in enumerate((wbuf, idbuf))
+    ]
+    start(shares)
     for n in range(LISTED):
         pt_t[:, n * SEGLEN : (n + 1) * SEGLEN] = pt[n * SEGLEN : (n + 1) * SEGLEN, :].T
     gcol[...] = jnp.broadcast_to(g, (128, g.shape[1])).T
@@ -247,12 +261,12 @@
         base_sum = base_sum + xbuf[d].astype(F32)
         kept_sum = kept_sum + lbuf[d].astype(F32)
     k = combine(k, lbuf)
-    all_of(wbuf, w_recv)
-    info = wbuf[:, LISTED : 2 * LISTED, :].astype(F32)
+    arrived(shares)
     per = 128 // LISTED
-    mine = iota((n_tm, LISTED, 128), 2) // LISTED == lax.rem(iota((n_tm, LISTED, 128), 0), per)
-    info = jnp.sum(jnp.where(mine, info, 0.0).reshape(n_tm // per, per, LISTED, 128), axis=1)
-    key = jnp.concatenate([info[c, 0:1] * 128.0 + info[c, 1:2] for c in range(n_tm // per)], axis=1)
+    mine = iota((n_tm, 128), 1) // LISTED == lax.rem(iota((n_tm, 128), 0), per)
+    spaced = jnp.where(mine, idbuf[...].reshape(n_tm, 128), 0.0).reshape(n_tm // per, per, 128)
+    spaced = jnp.sum(spaced, axis=1, keepdims=True)
+    key = jnp.concatenate([spaced[c] for c in range(n_tm // per)], axis=1)
     slot = det * n_tm + tm
     loads[9].wait()
     tile_mine = jnp.sum(
@@ -260,7 +274,7 @@
     )
     same = (own_key.astype(F32)[:, 0:1] == key).astype(F32).astype(BF16)
     into = (tile_mine * 128.0 + iota((128, listed), 0).astype(F32) == key).astype(F32).astype(BF16)
-    all_squares = wbuf[:, :LISTED, :].reshape(listed, TILE)
+    all_squares = wbuf[...].reshape(listed, TILE)
     own_scale = 1.0 / (1.0 + squared_gain * jnp.dot(same, all_squares, preferred_element_type=F32))
     tile_weight = 1.0 + squared_gain * jnp.dot(into, all_squares, preferred_element_type=F32)
     tile_scale = jnp.sqrt(tile_weight) / tile_weight
@@ -279,7 +293,7 @@
         parts.append(total)
     sig = jnp.concatenate(parts, axis=1)
     qbuf[0] = project(filter_rows(r - sig * k)[0:1]).astype(BF16)
-    spread(qbuf, q_send, q_recv)
+    spread(qbuf, q_send, q_recv, peers)
 
     amp = filter_rows(base_sum - sig * kept_sum)
     amp_high = amp.astype(BF16).astype(F32)
@@ -304,12 +318,21 @@
     sums = sums + jnp.dot(into, second, preferred_element_type=F32)
     tile_out[...] = sums * tile_scale
 
-    for copies in (x_copies, y_copies, l_copies, k_copies):
+    for copies in (x_copies, y_copies, l_copies, k_copies, shares):
         for copy in copies:
             copy.wait_send()
-    all_of(wbuf, w_send)
+    all_of(wbuf, w_send, half - 1)
+    all_of(idbuf, id_send, half - 1)
     all_of(pbuf, p_send)
     all_of(qbuf, q_send)
+
+
+def hand_out(tile, clean, tile_hbm, clean_hbm, sem):
+    copies = [pltpu.make_async_copy(tile, tile_hbm, sem.at[0]), pltpu.make_async_copy(clean, clean_hbm, sem.at[1])]
+    for copy in copies:
+        copy.start()
+    for copy in copies:
+        copy.wait()
 
 
 def solution(mesh):
@@ -352,14 +375,18 @@
                 pltpu.VMEM((n_det, MODES, samples), BF16),
                 pltpu.VMEM((n_det, MODES, samples), BF16),
                 pltpu.VMEM((n_det, 1, samples), F32),
-                pltpu.VMEM((n_tm, 2 * LISTED, TILE), BF16),
+                pltpu.VMEM((n_tm, LISTED, TILE), BF16),
+                pltpu.VMEM((n_tm, 1, 128), F32),
                 pltpu.VMEM((n_tm, LISTED, TILE), BF16),
                 pltpu.VMEM((n_tm, LISTED, TILE), BF16),
                 pltpu.SemaphoreType.REGULAR,
+                pltpu.SemaphoreType.REGULAR,
+                dma((2,)),
+                dma((2,)),
                 dma((10,)),
             ]
             + [dma((n_det - 1,))] * 8
-            + [dma] * 6,
+            + [dma] * 8,
             compiler_params=pltpu.CompilerParams(
                 collective_id=0, has_side_effects=True, vmem_limit_bytes=40 * 1024 * 1024
             ),
@@ -380,6 +407,16 @@
                 )
             )
         )
+        tile_snr, cleaned = pl.pallas_call(
+            hand_out,
+            out_shape=(
+                jax.ShapeDtypeStruct((TILE, TILE), F32),
+                jax.ShapeDtypeStruct((dets, samples), BF16),
+            ),
+            in_specs=[vmem, vmem],
+            out_specs=(hbm, hbm),
+            scratch_shapes=[dma((2,))],
+        )(*(pltpu.with_memory_space_constraint(x, pltpu.VMEM) for x in (tile_snr, cleaned)))
         return tile_snr.reshape(1, TILE, TILE), cleaned
 
     return jax.shard_map(

time: 25.4 us -> 24.9 us (0.980)
  local copies, waits for them, and re-layouts: 1.42 us -> 0 us
  Pallas kernels: 23.2 us -> 24.2 us
    unnamed x2 -> x0, local copies, waits for them, and re-layouts: 1.42 us -> none
    pallas_call x0 -> x1, Pallas kernels: none -> 0.83 us  [shards(): pl.pallas_call(hand_out, out_shape=(jax.ShapeDtypeStruct((TILE, TILE), F3...]
where the time goes in v4:
time: 24.9 us; the launch traced here: 24.8 us
  Pallas kernels  24.2 us (97%)
  between operations  0.64 us (3%)
    pallas_call x1, Pallas kernels, shards(): pl.pallas_call(functools.partial(kernel, n_det, n_tm), out_shape=(jax.Sha...  23.3 us
    pallas_call x1, Pallas kernels, shards(): pl.pallas_call(hand_out, out_shape=(jax.ShapeDtypeStruct((TILE, TILE), F3...  0.83 us

profile of v4, /device:TPU:1, one launch (start us, length us, event | category | flops | bytes accessed | tf_op | source)
XLA Modules:
  0.0 24.8 jit_solution(12327020692176106553)
XLA Ops:
  0.6 23.3 %shard_map.113 = (f32[128,128]{1,0:T(8,128)S(1)}, bf16[512,512]{1,0:T(8,128)(2,1)S(1)}) custom-call(f32[1,512]{1,0:T(1,128)} %bitcast.7, f32[32,512]{1,0:T(8,128)} %bitcast.6, s32[512,512]{1,0:T(8,128)} %fl_hbm.1, f32[512,512]{1,0:T(8,128)} %ts_hbm.1, bf16[2048,128]{1,0:T(8,128)(2,1)} %bitcast.5, s32[4,4]{1,0:T(4,128)} %tids_hbm.1, s32[4,4]{1,0:T(4,128)} %offs_hbm.1, ...), custom_call_target="tpu_custom_call" | custom-call | tf_op jit(solution)/shard_map/pallas_call | solution.py:349
  24.0 0.8 %shard_map.114 = (f32[128,128]{1,0:T(8,128)}, bf16[512,512]{1,0:T(8,128)(2,1)}) custom-call(f32[128,128]{1,0:T(8,128)S(1)} %get-tuple-element.6.tile, bf16[512,512]{1,0:T(8,128)(2,1)S(1)} %get-tuple-element.7.clean), custom_call_target="tpu_custom_call" | custom-call | tf_op jit(solution)/shard_map/pallas_call | solution.py:410

commit v5 on v4

--- a/solution.py
+++ b/solution.py
@@ -93,22 +93,12 @@
     for peer in near:
         pl.semaphore_signal(barrier, inc=1, device_id=peer, device_id_type=MESH)
 
-    def det_copies(buf, send, recv):
-        return [
+    def spread_det(buf, send, recv):
+        for d in (2, 1, 3):
             pltpu.make_async_remote_copy(
-                src_ref=buf.at[0], dst_ref=buf.at[d], send_sem=send.at[d - 1], recv_sem=recv.at[d - 1],
+                src_ref=buf.at[0], dst_ref=buf.at[d], send_sem=send, recv_sem=recv,
                 device_id=det_peers[d - 1], device_id_type=MESH,
-            )
-            for d in range(1, n_det)
-        ]
-
-    def start(copies):
-        for copy in copies:
-            copy.start()
-
-    def arrived(copies):
-        for copy in copies:
-            copy.wait_recv()
+            ).start()
 
     def spread(buf, send, recv, to):
         for d, peer in to:
@@ -117,7 +107,7 @@
                 device_id=peer, device_id_type=MESH,
             ).start()
 
-    def all_of(buf, sem, count=n_tm - 1):
+    def all_of(buf, sem, count):
         rest = buf.at[pl.ds(1, count)]
         pltpu.make_async_copy(rest, rest, sem).wait()
 
@@ -146,10 +136,8 @@
     pl.semaphore_wait(barrier, len(near))
     for peer in row_peers:
         pl.semaphore_signal(column_sem, inc=1, device_id=peer, device_id_type=MESH)
-    x_copies = det_copies(xbuf, x_send, x_recv)
-    y_copies = det_copies(ybuf, y_send, y_recv)
-    start(x_copies)
-    start(y_copies)
+    spread_det(xbuf, x_send, x_recv)
+    spread_det(ybuf, y_send, y_recv)
 
     for n in (4, 5, 6):
         loads[n].wait()
@@ -173,10 +161,8 @@
     kept = folded(jnp.dot(halves(weights * g), keepb[...], preferred_element_type=F32))
     lbuf[0] = kept[:MODES].astype(BF16)
     kbuf[0] = kept[MODES : MODES + 1]
-    l_copies = det_copies(lbuf, l_send, l_recv)
-    k_copies = det_copies(kbuf, k_send, k_recv)
-    start(l_copies)
-    start(k_copies)
+    spread_det(lbuf, l_send, l_recv)
+    spread_det(kbuf, k_send, k_recv)
 
     loads[8].wait()
     gain = fgain[...].reshape(1, HALF + 1)
@@ -217,8 +203,8 @@
         lhs = jnp.concatenate(rows, axis=0).astype(BF16)
         return folded(jnp.dot(lhs, pt[...], preferred_element_type=F32))
 
-    arrived(x_copies)
-    arrived(y_copies)
+    all_of(xbuf, x_recv, n_det - 1)
+    all_of(ybuf, y_recv, n_det - 1)
     y = ybuf[0]
     for d in range(1, n_det):
         y = y + ybuf[d]
@@ -244,15 +230,16 @@
         )
         for n, buf in enumerate((wbuf, idbuf))
     ]
-    start(shares)
+    for copy in shares:
+        copy.start()
     for n in range(LISTED):
         pt_t[:, n * SEGLEN : (n + 1) * SEGLEN] = pt[n * SEGLEN : (n + 1) * SEGLEN, :].T
     gcol[...] = jnp.broadcast_to(g, (128, g.shape[1])).T
     vt_high = vt.astype(BF16).astype(F32)
     vt_low = vt - vt_high
     vcat[...] = jnp.concatenate([vt_high, vt_low, vt_high, jnp.zeros_like(vt)], axis=0).T.astype(BF16)
-    arrived(l_copies)
-    arrived(k_copies)
+    all_of(lbuf, l_recv, n_det - 1)
+    all_of(kbuf, k_recv, n_det - 1)
     k = kbuf[0]
     base_sum = xbuf[0].astype(F32)
     kept_sum = lbuf[0].astype(F32)
@@ -261,7 +248,8 @@
         base_sum = base_sum + xbuf[d].astype(F32)
         kept_sum = kept_sum + lbuf[d].astype(F32)
     k = combine(k, lbuf)
-    arrived(shares)
+    for copy in shares:
+        copy.wait_recv()
     per = 128 // LISTED
     mine = iota((n_tm, 128), 1) // LISTED == lax.rem(iota((n_tm, 128), 0), per)
     spaced = jnp.where(mine, idbuf[...].reshape(n_tm, 128), 0.0).reshape(n_tm // per, per, 128)
@@ -279,7 +267,7 @@
     tile_weight = 1.0 + squared_gain * jnp.dot(into, all_squares, preferred_element_type=F32)
     tile_scale = jnp.sqrt(tile_weight) / tile_weight
 
-    all_of(pbuf, p_recv)
+    all_of(pbuf, p_recv, n_tm - 1)
     first = pbuf[...].reshape(listed, TILE)
     fetched = (jnp.dot(same, first, preferred_element_type=F32) * own_scale).astype(BF16)
     wide = jnp.dot(fetched, pt_t[...], preferred_element_type=F32)
@@ -313,18 +301,19 @@
     lax.fori_loop(0, ts.shape[0] // chunk, clean_rows, 0)
     sums = jnp.dot(into, first, preferred_element_type=F32)
 
-    all_of(qbuf, q_recv)
+    all_of(qbuf, q_recv, n_tm - 1)
     second = qbuf[...].reshape(listed, TILE)
     sums = sums + jnp.dot(into, second, preferred_element_type=F32)
     tile_out[...] = sums * tile_scale
 
-    for copies in (x_copies, y_copies, l_copies, k_copies, shares):
-        for copy in copies:
-            copy.wait_send()
+    for buf, sem in ((xbuf, x_send), (ybuf, y_send), (lbuf, l_send), (kbuf, k_send)):
+        all_of(buf, sem, n_det - 1)
+    for copy in shares:
+        copy.wait_send()
     all_of(wbuf, w_send, half - 1)
     all_of(idbuf, id_send, half - 1)
-    all_of(pbuf, p_send)
-    all_of(qbuf, q_send)
+    all_of(pbuf, p_send, n_tm - 1)
+    all_of(qbuf, q_send, n_tm - 1)
 
 
 def hand_out(tile, clean, tile_hbm, clean_hbm, sem):
@@ -385,8 +374,7 @@
                 dma((2,)),
                 dma((10,)),
             ]
-            + [dma((n_det - 1,))] * 8
-            + [dma] * 8,
+            + [dma] * 16,
             compiler_params=pltpu.CompilerParams(
                 collective_id=0, has_side_effects=True, vmem_limit_bytes=40 * 1024 * 1024
             ),

time: 24.9 us -> 24.7 us (level)
  no operation moved by 1% of the time
where the time goes in v5:
time: 24.7 us; the launch traced here: 24.6 us
  Pallas kernels  24 us (97%)
  between operations  0.64 us (3%)
    pallas_call x1, Pallas kernels, shards(): pl.pallas_call(functools.partial(kernel, n_det, n_tm), out_shape=(jax.Sha...  23.1 us
    pallas_call x1, Pallas kernels, shards(): pl.pallas_call(hand_out, out_shape=(jax.ShapeDtypeStruct((TILE, TILE), F3...  0.83 us

profile of v5, /device:TPU:1, one launch (start us, length us, event | category | flops | bytes accessed | tf_op | source)
XLA Modules:
  0.0 24.6 jit_solution(2176092037600732875)
XLA Ops:
  0.6 23.1 %shard_map.113 = (f32[128,128]{1,0:T(8,128)S(1)}, bf16[512,512]{1,0:T(8,128)(2,1)S(1)}) custom-call(f32[1,512]{1,0:T(1,128)} %bitcast.7, f32[32,512]{1,0:T(8,128)} %bitcast.6, s32[512,512]{1,0:T(8,128)} %fl_hbm.1, f32[512,512]{1,0:T(8,128)} %ts_hbm.1, bf16[2048,128]{1,0:T(8,128)(2,1)} %bitcast.5, s32[4,4]{1,0:T(4,128)} %tids_hbm.1, s32[4,4]{1,0:T(4,128)} %offs_hbm.1, ...), custom_call_target="tpu_custom_call" | custom-call | tf_op jit(solution)/shard_map/pallas_call | solution.py:338
  23.8 0.8 %shard_map.114 = (f32[128,128]{1,0:T(8,128)}, bf16[512,512]{1,0:T(8,128)(2,1)}) custom-call(f32[128,128]{1,0:T(8,128)S(1)} %get-tuple-element.6.tile, bf16[512,512]{1,0:T(8,128)(2,1)S(1)} %get-tuple-element.7.clean), custom_call_target="tpu_custom_call" | custom-call | tf_op jit(solution)/shard_map/pallas_call | solution.py:398

commit v6 on v5

--- a/solution.py
+++ b/solution.py
@@ -61,6 +61,11 @@
     det, tm = lax.axis_index("det"), lax.axis_index("tm")
     listed = n_tm * LISTED
 
+    det_peers = [{"det": lax.rem(det + d, n_det)} for d in range(1, n_det)]
+    barrier = pltpu.get_barrier_semaphore()
+    for peer in det_peers:
+        pl.semaphore_signal(barrier, inc=1, device_id=peer, device_id_type=MESH)
+
     loads = []
     pairs = (
         (gains_hbm, gains), (modes_hbm, modes), (fl_hbm, fl), (ts_hbm, ts), (pt_hbm, pt),
@@ -82,14 +87,12 @@
             lax.rem(tm_x + dx, n_x) * (2 * n_z) + lax.rem(tm_z + dz, n_z) * 2 + lax.rem(tm_core + dc, 2)
         )
         peers.append((dc * half + dx * n_z + dz, {"tm": peer}))
-    det_peers = [{"det": lax.rem(det + d, n_det)} for d in range(1, n_det)]
-
-    barrier = pltpu.get_barrier_semaphore()
     row_peers = [peer for (_, dz, dc), (_, peer) in zip(offsets, peers) if dz == 0 and dc == 0]
     column_peers = [peer for (dx, _, dc), (_, peer) in zip(offsets, peers) if dx == 0 and dc == 0]
+    across = sorted(((dx, dc) for dx in range(n_x) for dc in range(2)), key=lambda o: -(min(o[0], n_x - o[0]) * 2 + o[1]))
     plane_peers = [pair for (_, _, dc), pair in zip(offsets, peers) if dc == 0]
     sibling = {"tm": tm + 1 - 2 * tm_core}
-    near = column_peers + det_peers + row_peers + [sibling]
+    near = column_peers + row_peers + [sibling]
     for peer in near:
         pl.semaphore_signal(barrier, inc=1, device_id=peer, device_id_type=MESH)
 
@@ -106,6 +109,26 @@
                 src_ref=buf.at[0], dst_ref=buf.at[d], send_sem=send, recv_sem=recv,
                 device_id=peer, device_id_type=MESH,
             ).start()
+
+    def spread_rows(buf, send, recv, targets):
+        for z in targets:
+            dz = lax.rem(z - tm_z + n_z, n_z)
+            for dx, dc in across:
+                slot = dc * half + dx * n_z + dz
+                peer = (
+                    lax.rem(tm_x + dx, n_x) * (2 * n_z) + z * 2 + lax.rem(tm_core + dc, 2)
+                )
+
+                def send_one(slot=slot, peer=peer):
+                    pltpu.make_async_remote_copy(
+                        src_ref=buf.at[0], dst_ref=buf.at[slot], send_sem=send, recv_sem=recv,
+                        device_id={"tm": peer}, device_id_type=MESH,
+                    ).start()
+
+                if dx == 0 and dc == 0:
+                    pl.when(dz != 0)(send_one)
+                else:
+                    send_one()
 
     def all_of(buf, sem, count):
         rest = buf.at[pl.ds(1, count)]
@@ -133,11 +156,11 @@
     base = folded(jnp.dot(weight_halves, residual, preferred_element_type=F32))
     xbuf[0] = base[:MODES].astype(BF16)
     ybuf[0] = jnp.concatenate([base[MODES : MODES + 1], jnp.concatenate([copies_u, squared], axis=1)], axis=0)
-    pl.semaphore_wait(barrier, len(near))
+    pl.semaphore_wait(barrier, len(det_peers) + len(near))
+    spread_det(xbuf, x_send, x_recv)
+    spread_det(ybuf, y_send, y_recv)
     for peer in row_peers:
         pl.semaphore_signal(column_sem, inc=1, device_id=peer, device_id_type=MESH)
-    spread_det(xbuf, x_send, x_recv)
-    spread_det(ybuf, y_send, y_recv)
 
     for n in (4, 5, 6):
         loads[n].wait()
@@ -193,15 +216,12 @@
 
     def project(z):
         z_high = z.astype(BF16).astype(F32)
-        rows = []
-        for part in (z_high, z - z_high):
-            blocks = []
-            for n in range(LISTED):
-                s = n // KBLK
-                blocks.append(jnp.where(row16 == n, part[:, s * SEGLEN : (s + 1) * SEGLEN], 0.0))
-            rows.append(jnp.concatenate(blocks, axis=1))
-        lhs = jnp.concatenate(rows, axis=0).astype(BF16)
-        return folded(jnp.dot(lhs, pt[...], preferred_element_type=F32))
+        blocks = []
+        for n in range(LISTED):
+            s = n // KBLK
+            blocks.append(jnp.where(row16 == n, z_high[:, s * SEGLEN : (s + 1) * SEGLEN], 0.0))
+        lhs = jnp.concatenate(blocks, axis=1).astype(BF16)
+        return jnp.dot(lhs, pt[...], preferred_element_type=F32)
 
     all_of(xbuf, x_recv, n_det - 1)
     all_of(ybuf, y_recv, n_det - 1)
@@ -219,7 +239,7 @@
     r = combine(y[0:1], xbuf)
     pbuf[0] = project(filter_rows(r)[0:1]).astype(BF16)
     pl.semaphore_wait(core_sem, 1)
-    spread(pbuf, p_send, p_recv, peers)
+    spread_rows(pbuf, p_send, p_recv, (2, 1, 3, 0))
 
     all_of(wbuf, w_recv, half - 1)
     all_of(idbuf, id_recv, half - 1)
@@ -281,7 +301,7 @@
         parts.append(total)
     sig = jnp.concatenate(parts, axis=1)
     qbuf[0] = project(filter_rows(r - sig * k)[0:1]).astype(BF16)
-    spread(qbuf, q_send, q_recv, peers)
+    spread_rows(qbuf, q_send, q_recv, (0, 1, 3, 2))
 
     amp = filter_rows(base_sum - sig * kept_sum)
     amp_high = amp.astype(BF16).astype(F32)

time: 24.7 us -> 24.5 us (level)
  Pallas kernels: 24 us -> 23.7 us
where the time goes in v6:
time: 24.5 us; the launch traced here: 24.3 us
  Pallas kernels  23.7 us (97%)
  between operations  0.64 us (3%)
    pallas_call x1, Pallas kernels, shards(): pl.pallas_call(functools.partial(kernel, n_det, n_tm), out_shape=(jax.Sha...  22.9 us
    pallas_call x1, Pallas kernels, shards(): pl.pallas_call(hand_out, out_shape=(jax.ShapeDtypeStruct((TILE, TILE), F3...  0.83 us

profile of v6, /device:TPU:1, one launch (start us, length us, event | category | flops | bytes accessed | tf_op | source)
XLA Modules:
  0.0 24.3 jit_solution(8694184535044488744)
XLA Ops:
  0.6 22.9 %shard_map.113 = (f32[128,128]{1,0:T(8,128)S(1)}, bf16[512,512]{1,0:T(8,128)(2,1)S(1)}) custom-call(f32[1,512]{1,0:T(1,128)} %bitcast.7, f32[32,512]{1,0:T(8,128)} %bitcast.6, s32[512,512]{1,0:T(8,128)} %fl_hbm.1, f32[512,512]{1,0:T(8,128)} %ts_hbm.1, bf16[2048,128]{1,0:T(8,128)(2,1)} %bitcast.5, s32[4,4]{1,0:T(4,128)} %tids_hbm.1, s32[4,4]{1,0:T(4,128)} %offs_hbm.1, ...), custom_call_target="tpu_custom_call" | custom-call | tf_op jit(solution)/shard_map/pallas_call | solution.py:358
  23.5 0.8 %shard_map.114 = (f32[128,128]{1,0:T(8,128)}, bf16[512,512]{1,0:T(8,128)(2,1)}) custom-call(f32[128,128]{1,0:T(8,128)S(1)} %get-tuple-element.6.tile, bf16[512,512]{1,0:T(8,128)(2,1)S(1)} %get-tuple-element.7.clean), custom_call_target="tpu_custom_call" | custom-call | tf_op jit(solution)/shard_map/pallas_call | solution.py:418

commit v7 on v6

--- a/solution.py
+++ b/solution.py
@@ -216,12 +216,15 @@
 
     def project(z):
         z_high = z.astype(BF16).astype(F32)
-        blocks = []
-        for n in range(LISTED):
-            s = n // KBLK
-            blocks.append(jnp.where(row16 == n, z_high[:, s * SEGLEN : (s + 1) * SEGLEN], 0.0))
-        lhs = jnp.concatenate(blocks, axis=1).astype(BF16)
-        return jnp.dot(lhs, pt[...], preferred_element_type=F32)
+        rows = []
+        for part in (z_high, z - z_high):
+            blocks = []
+            for n in range(LISTED):
+                s = n // KBLK
+                blocks.append(jnp.where(row16 == n, part[:, s * SEGLEN : (s + 1) * SEGLEN], 0.0))
+            rows.append(jnp.concatenate(blocks, axis=1))
+        lhs = jnp.concatenate(rows, axis=0).astype(BF16)
+        return folded(jnp.dot(lhs, pt[...], preferred_element_type=F32))
 
     all_of(xbuf, x_recv, n_det - 1)
     all_of(ybuf, y_recv, n_det - 1)

time: 24.5 us -> 24.5 us (level)
  no operation moved by 1% of the time
where the time goes in v7:
time: 24.5 us; the launch traced here: 24.4 us
  Pallas kernels  23.8 us (97%)
  between operations  0.64 us (3%)
    pallas_call x1, Pallas kernels, shards(): pl.pallas_call(functools.partial(kernel, n_det, n_tm), out_shape=(jax.Sha...  22.9 us
    pallas_call x1, Pallas kernels, shards(): pl.pallas_call(hand_out, out_shape=(jax.ShapeDtypeStruct((TILE, TILE), F3...  0.83 us

profile of v7, /device:TPU:1, one launch (start us, length us, event | category | flops | bytes accessed | tf_op | source)
XLA Modules:
  0.0 24.4 jit_solution(2973494438225822659)
XLA Ops:
  0.6 22.9 %shard_map.113 = (f32[128,128]{1,0:T(8,128)S(1)}, bf16[512,512]{1,0:T(8,128)(2,1)S(1)}) custom-call(f32[1,512]{1,0:T(1,128)} %bitcast.7, f32[32,512]{1,0:T(8,128)} %bitcast.6, s32[512,512]{1,0:T(8,128)} %fl_hbm.1, f32[512,512]{1,0:T(8,128)} %ts_hbm.1, bf16[2048,128]{1,0:T(8,128)(2,1)} %bitcast.5, s32[4,4]{1,0:T(4,128)} %tids_hbm.1, s32[4,4]{1,0:T(4,128)} %offs_hbm.1, ...), custom_call_target="tpu_custom_call" | custom-call | tf_op jit(solution)/shard_map/pallas_call | solution.py:361
  23.6 0.8 %shard_map.114 = (f32[128,128]{1,0:T(8,128)}, bf16[512,512]{1,0:T(8,128)(2,1)}) custom-call(f32[128,128]{1,0:T(8,128)S(1)} %get-tuple-element.6.tile, bf16[512,512]{1,0:T(8,128)(2,1)S(1)} %get-tuple-element.7.clean), custom_call_target="tpu_custom_call" | custom-call | tf_op jit(solution)/shard_map/pallas_call | solution.py:421
